TPU v7x, 256 devices: a whole 4x4x8 slice. The times are simulated.
256 devices in a mesh: rows: 64 (over y, z, core), cents: 4 (over x).
Axes of the slice: x: 4, y: 4, z: 8, core: 2. Of those that a mesh axis runs over, the one named last changes fastest.
Arguments:
- patients: bfloat16 [131072, 256], P('rows')
- centroids: bfloat16 [8192, 256], P('cents'), as said below
Outputs:
- new_centroids: float32 [8192, 256], P('cents')
- log_scale: float32 [131072], P('rows')
Inputs may be any that keep to these rules, and one draw needn't show every extreme that they name: `centroids`: centroid embeddings.
All inputs are finite; a program needn't handle non-finite values.
Results may differ from a plain program's by a relative error of at most 0.002.
Values sent between devices are 32-bit elements; how exact they have to be, the bound alone decides.
A program may use at most 64 MiB of HBM per device.

v0:
```python
import jax
import jax.numpy as jnp
from jax import lax
from jax.sharding import PartitionSpec as P

ITERS = 3


TAU = 0.05


def local(patients, centroids):
    row_count = patients.shape[0]
    cent_count = centroids.shape[0]
    ratio = jnp.float32(row_count * lax.axis_size("rows") / (cent_count * lax.axis_size("cents")))
    cent_f = centroids.astype(jnp.float32)
    norms = jnp.sum(cent_f * cent_f, axis=1)
    scores = lax.dot_general(
        patients, centroids, (((1,), (1,)), ((), ())), preferred_element_type=jnp.float32
    )
    logits = (2.0 * scores - norms[None, :]) / TAU
    peak = lax.pmax(jnp.max(logits, axis=1), "cents")
    expo = jnp.exp(logits - peak[:, None])
    row_scale = jnp.ones((row_count,), jnp.float32)
    col_scale = jnp.ones((cent_count,), jnp.float32)
    for step in range(ITERS):
        column_mass = lax.psum(jnp.sum(expo * row_scale[:, None], axis=0), "rows")
        col_scale = ratio / jnp.maximum(column_mass, 1.0)
        row_mass = lax.psum(jnp.sum(expo * col_scale[None, :], axis=1), "cents")
        row_scale = 1.0 / row_mass
    assign = expo * row_scale[:, None] * col_scale[None, :]
    weight_local = jnp.sum(assign, axis=0)
    assign_low = assign.astype(jnp.bfloat16)
    numer_local = lax.dot_general(
        assign_low, patients, (((0,), (0,)), ((), ())), preferred_element_type=jnp.float32
    )
    numer, weight = lax.psum((numer_local, weight_local), "rows")
    new_centroids = numer / jnp.maximum(weight, 1.0)[:, None]
    return (new_centroids, jnp.log(row_scale))


def solution(mesh):
    return jax.shard_map(
        local,
        mesh=mesh,
        in_specs=(P("rows", None), P("cents", None)),
        out_specs=(P("cents", None), P("rows")),
        check_vma=False,
    )
```

profile of v0, /device:TPU:1, one launch (start us, length us, event | category | flops | bytes accessed | tf_op | source)
XLA Modules:
  0.0 691.7 jit_solution(1310871066561602554)
XLA Ops:
  7.2 0.0 copy-start
  7.2 0.0 all-reduce.2.cloned.1.call-start
  7.2 1.6 multiply_reduce_fusion.5
  8.9 0.0 copy-done
  8.9 8.3 %fusion.2 = (f32[2048]{0:T(1024)S(1)}, f32[2048,2048]{1,0:T(8,128)}) fusion(f32[2048]{0:T(1024)S(1)} %multiply_reduce_fusion.5, bf16[2048,256]{1,0:T(8,128)(2,1)S(1)} %copy-done, bf16[2048,256]{1,0:T(8,128)(2,1)} %param.3), kind=kOutput, calls=%fused_computation.10 | convolution fusion | flops 2164258816 | bytes 18890752 | tf_op jit(solution)/shard_map/dot_general | solution.py:18
  17.1 9.4 %pmax.7 = f32[2048]{0:T(1024)S(1)} all-reduce(f32[2048]{0:T(1024)S(1)} %get-tuple-element.4), channel_id=1, replica_groups=mesh['rows'=64,'cents'=4] {'cents'}, use_global_device_ids=true, to_apply=%region_2.0 | all-reduce | flops 2048 | bytes 16384 | tf_op jit(solution)/shard_map/pmax | solution.py:22
  26.5 8.2 %fusion.8 = f32[2048]{0:T(1024)S(1)} fusion(f32[2048]{0:T(1024)S(1)} %pmax.7, f32[2048]{0:T(1024)S(1)} %multiply_reduce_fusion.5, f32[2048,2048]{1,0:T(8,128)} %get-tuple-element.5), kind=kLoop, calls=%fused_computation.24 | loop fusion | flops 20969472 | bytes 16801792 | tf_op jit(solution)/shard_map/reduce_sum | solution.py:27
  34.7 131.5 %psum.56 = f32[2048]{0:T(1024)S(1)} all-reduce(f32[2048]{0:T(1024)S(1)} %fusion.8), channel_id=1, replica_groups=mesh['rows'=64,'cents'=4] {'rows'}, use_global_device_ids=true, to_apply=%region_4.0 | all-reduce | flops 2048 | bytes 16384 | tf_op jit(solution)/shard_map/psum | solution.py:27
  166.2 8.5 %multiply_reduce_fusion.4 = f32[2048]{0:T(1024)S(1)} fusion(f32[2048]{0:T(1024)S(1)} %maximum_divide_fusion.2, f32[2048]{0:T(1024)S(1)} %pmax.7, f32[2048]{0:T(1024)S(1)} %multiply_reduce_fusion.5, f32[2048,2048]{1,0:T(8,128)} %get-tuple-element.5), kind=kLoop, calls=%fused_computation.5 | loop fusion | flops 25163776 | bytes 16809984 | tf_op jit(solution)/shard_map/reduce_sum | solution.py:29
  174.8 6.1 psum.57
  180.9 8.3 %multiply_reduce_fusion.3 = f32[2048]{0:T(1024)S(1)} fusion(f32[2048]{0:T(1024)S(1)} %broadcast_divide_fusion.3, f32[2048]{0:T(1024)S(1)} %pmax.7, f32[2048]{0:T(1024)S(1)} %multiply_reduce_fusion.5, f32[2048,2048]{1,0:T(8,128)} %get-tuple-element.5), kind=kLoop, calls=%fused_computation.4 | loop fusion | flops 25163776 | bytes 16809984 | tf_op jit(solution)/shard_map/reduce_sum | solution.py:27
  189.2 130.2 %psum.58 = f32[2048]{0:T(1024)S(1)} all-reduce(f32[2048]{0:T(1024)S(1)} %multiply_reduce_fusion.3), channel_id=1, replica_groups=mesh['rows'=64,'cents'=4] {'rows'}, use_global_device_ids=true, to_apply=%region_8.0 | all-reduce | flops 2048 | bytes 16384 | tf_op jit(solution)/shard_map/psum | solution.py:27
  319.4 8.5 %multiply_reduce_fusion.2 = f32[2048]{0:T(1024)S(1)} fusion(f32[2048]{0:T(1024)S(1)} %maximum_divide_fusion.1, f32[2048]{0:T(1024)S(1)} %pmax.7, f32[2048]{0:T(1024)S(1)} %multiply_reduce_fusion.5, f32[2048,2048]{1,0:T(8,128)} %get-tuple-element.5), kind=kLoop, calls=%fused_computation.3 | loop fusion | flops 25163776 | bytes 16809984 | tf_op jit(solution)/shard_map/reduce_sum | solution.py:29
  327.9 7.8 %psum.59 = f32[2048]{0:T(1024)S(1)} all-reduce(f32[2048]{0:T(1024)S(1)} %multiply_reduce_fusion.2), channel_id=1, replica_groups=mesh['rows'=64,'cents'=4] {'cents'}, use_global_device_ids=true, to_apply=%region_10.0 | all-reduce | flops 2048 | bytes 16384 | tf_op jit(solution)/shard_map/psum | solution.py:29
  335.8 8.3 %multiply_reduce_fusion.1 = f32[2048]{0:T(1024)S(1)} fusion(f32[2048]{0:T(1024)S(1)} %broadcast_divide_fusion.2, f32[2048]{0:T(1024)S(1)} %pmax.7, f32[2048]{0:T(1024)S(1)} %multiply_reduce_fusion.5, f32[2048,2048]{1,0:T(8,128)} %get-tuple-element.5), kind=kLoop, calls=%fused_computation.2 | loop fusion | flops 25163776 | bytes 16809984 | tf_op jit(solution)/shard_map/reduce_sum | solution.py:27
  344.1 128.1 %psum.60 = f32[2048]{0:T(1024)S(1)} all-reduce(f32[2048]{0:T(1024)S(1)} %multiply_reduce_fusion.1), channel_id=1, replica_groups=mesh['rows'=64,'cents'=4] {'rows'}, use_global_device_ids=true, to_apply=%region_12.0 | all-reduce | flops 2048 | bytes 16384 | tf_op jit(solution)/shard_map/psum | solution.py:27
  472.2 8.5 %multiply_reduce_fusion = f32[2048]{0:T(1024)S(1)} fusion(f32[2048]{0:T(1024)S(1)} %maximum_divide_fusion, f32[2048]{0:T(1024)S(1)} %pmax.7, f32[2048]{0:T(1024)S(1)} %multiply_reduce_fusion.5, f32[2048,2048]{1,0:T(8,128)} %get-tuple-element.5), kind=kLoop, calls=%fused_computation.1 | loop fusion | flops 25163776 | bytes 16809984 | tf_op jit(solution)/shard_map/reduce_sum | solution.py:29
  480.7 6.3 psum.61
  487.0 0.6 fusion.7
  487.6 11.1 %fusion.3 = f32[2048,256]{1,0:T(8,128)} fusion(bf16[2048,256]{1,0:T(8,128)(2,1)S(1)} %copy-done, f32[2048]{0:T(1024)S(1)} %get-tuple-element.3, f32[2048]{0:T(1024)S(1)} %maximum_divide_fusion, f32[2048,2048]{1,0:T(8,128)} %get-tuple-element.5, f32[2048]{0:T(1024)S(1)} %pmax.7, f32[2048]{0:T(1024)S(1)} %multiply_reduce_fusion.5), kind=kOutput, calls=%fused_computation.11 | convolution fusion | flops 2176843776 | bytes 19955712 | tf_op jit(solution)/shard_map/dot_general | solution.py:34
  498.7 0.0 all-reduce.2.cloned.1.call-update
  498.8 8.8 %fusion = f32[2048]{0:T(1024)S(1)} fusion(f32[2048]{0:T(1024)S(1)} %get-tuple-element.3, f32[2048]{0:T(1024)S(1)} %maximum_divide_fusion, f32[2048]{0:T(1024)S(1)} %pmax.7, f32[2048]{0:T(1024)S(1)} %multiply_reduce_fusion.5, f32[2048,2048]{1,0:T(8,128)} %get-tuple-element.5), kind=kLoop, calls=%fused_computation.8 | loop fusion | flops 29358080 | bytes 16818176 | tf_op jit(solution)/shard_map/reduce_sum | solution.py:32
  507.5 128.0 %psum.63 = f32[2048]{0:T(1024)S(1)} all-reduce(f32[2048]{0:T(1024)S(1)} %fusion), channel_id=1, replica_groups=mesh['rows'=64,'cents'=4] {'rows'}, use_global_device_ids=true, to_apply=%region_17.0 | all-reduce | flops 2048 | bytes 16384 | tf_op jit(solution)/shard_map/psum | solution.py:37
  635.5 46.1 %all-reduce.2.cloned.1.call-done = f32[2048,256]{1,0:T(8,128)} async-done(((f32[2048,256]{1,0:T(8,128)}), f32[2048,256]{1,0:T(8,128)}) %all-reduce.2.cloned.1.call-update) | async-done | bytes 2097168 | tf_op jit(solution)/shard_map/psum | solution.py:37
  681.6 3.3 broadcast_divide_fusion
  (6 shorter events, 0.0 us)
Async XLA Ops:
  7.2 1.7 copy-start
  7.2 674.5 %all-reduce.2.cloned.1.call-start = ((), (), s32[]{:S(2)}) async-start(), calls=%async_computation | async-start | bytes 4194304 | tf_op jit(solution)/shard_map/psum | solution.py:37
Sparse Core Ops, SparseCore 0:
  498.9 182.7 all-reduce.1
where the time goes:
time: 693 us; the launch traced here: 692 us
  blocking collectives  547 us (79%)
  other arithmetic  64.6 us (9%)
  waiting for transfers between devices  46.1 us (7%)
  matrix products  19.4 us (3%)
  between operations  14.2 us (2%)
    psum x3, blocking collectives, local(): column_mass = lax.psum(jnp.sum(expo * row_scale[:, None], axis=0), 'rows')  390 us
    psum x1, blocking collectives, local(): numer, weight = lax.psum((numer_local, weight_local), 'rows')  128 us
    psum x1, waiting for transfers between devices, local(): numer, weight = lax.psum((numer_local, weight_local), 'rows')  46.1 us
    reduce_sum x3, other arithmetic, local(): row_mass = lax.psum(jnp.sum(expo * col_scale[None, :], axis=1), 'cents')  25.5 us
    reduce_sum x3, other arithmetic, local(): column_mass = lax.psum(jnp.sum(expo * row_scale[:, None], axis=0), 'rows')  24.8 us
    psum x3, blocking collectives, local(): row_mass = lax.psum(jnp.sum(expo * col_scale[None, :], axis=1), 'cents')  20.2 us
  transfers between devices with their start and end apart: 1, of which 1 were waited for; matrix products, arithmetic and copies ran while one was open for 1% of the time, Pallas kernels for 0%

commit v1 on v0

v1 whole, which is shorter than its diff:
```python
import functools
import math

import jax
import jax.numpy as jnp
from jax import lax
from jax.experimental import pallas as pl
from jax.experimental.pallas import tpu as pltpu
from jax.sharding import PartitionSpec as P

ITERS = 3
TAU = 0.05
LOG2E = math.log2(math.e)

NX, NY, NZ = 4, 4, 8
R = 2048
K = 2048
D = 256
HALF = K // 2
GROUP = HALF // NZ
SHARD = GROUP // NY
LANES = 128
CHUNKS = R // LANES
MESH = pl.DeviceIdType.MESH
NT = (((1,), (1,)), ((), ()))


def far_first(i):
    half = (i + 1) // 2
    return 4 + half * (1 - 2 * lax.rem(i, 2))


def kernel(
    ratio, p_ref, c_ref, new_ref, log_ref,
    expo, col_b, row_b, acc, norm_b, peak8, factor,
    dense, pre, own, colbuf, total, rowpart, xbuf,
    low, numer, corebuf, ybuf, zsrc, zbuf,
    pre_s, pre_r, col_s, col_r, post_s, post_r, x_s, x_r,
    core_s, core_r, y_s, y_r, z_s, z_r, agz_s, agz_r, agy_s, agy_r, agc_s, agc_r,
):
    x = lax.axis_index("cents")
    rows = lax.axis_index("rows")
    core = lax.rem(rows, 2)
    z = lax.rem(rows // 2, NZ)
    y = rows // (2 * NZ)
    other = 1 - core

    def dev(dx=0, dy=0, dz=0, flip=False):
        yy = lax.rem(y + dy, NY)
        zz = lax.rem(z + dz, NZ)
        cc = other if flip else core
        return {"rows": (yy * NZ + zz) * 2 + cc, "cents": lax.rem(x + dx, NX)}

    def copy(src, dst, send, recv, to):
        return pltpu.make_async_remote_copy(
            src_ref=src, dst_ref=dst, send_sem=send, recv_sem=recv, device_id=to, device_id_type=MESH
        )

    barrier = pltpu.get_barrier_semaphore()

    def greet(i, carry):
        dz = far_first(i)
        for dy in (2, 1, 3):
            pl.semaphore_signal(barrier, inc=1, device_id=dev(dy=dy, dz=dz), device_id_type=MESH)

        @pl.when(i < NZ - 1)
        def _():
            pl.semaphore_signal(barrier, inc=1, device_id=dev(dz=dz), device_id_type=MESH)

        return carry

    lax.fori_loop(0, NZ, greet, 0)
    for dx in (2, 1, 3):
        pl.semaphore_signal(barrier, inc=1, device_id=dev(dx=dx), device_id_type=MESH)
    pl.semaphore_signal(barrier, inc=1, device_id=dev(flip=True), device_id_type=MESH)

    def norms(q, carry):
        at = pl.ds(pl.multiple_of(q * 256, 256), 256)
        cent = c_ref[at, :].astype(jnp.float32)
        norm_b[at, :] = jnp.broadcast_to(
            jnp.sum(cent * cent, axis=1, keepdims=True) * (LOG2E / TAU), (256, LANES)
        )
        return carry

    lax.fori_loop(0, K // 256, norms, 0)

    def scores(b, carry):
        lanes = pl.ds(pl.multiple_of(b * 256, 256), 256)
        block = p_ref[lanes, :]

        def part(q, top):
            at = pl.ds(pl.multiple_of(q * 512, 512), 512)
            s = lax.dot_general(c_ref[at, :], block, NT, preferred_element_type=jnp.float32)
            bias = norm_b[at, :]
            t = s * (2.0 * LOG2E / TAU) - jnp.concatenate([bias, bias], axis=1)
            expo[at, lanes] = t
            return jnp.maximum(top, jnp.max(t.reshape(64, 8, 256), axis=0))

        top = lax.fori_loop(0, K // 512, part, jnp.full((8, 256), -jnp.inf, jnp.float32))
        top = jnp.max(top, axis=0, keepdims=True)
        peak8[:, lanes] = jnp.broadcast_to(top, (8, 256))
        return carry

    lax.fori_loop(0, R // 256, scores, 0)

    def exps(q, carry):
        at = pl.ds(pl.multiple_of(q * 8, 8), 8)
        for k in range(CHUNKS):
            lanes = slice(k * LANES, (k + 1) * LANES)
            expo[at, lanes] = jnp.exp2(expo[at, lanes] - peak8[:, lanes])
        return carry

    lax.fori_loop(0, K // 8, exps, 0, unroll=4)

    def to_dense(src8, dst):
        for g in range(CHUNKS):
            dst[g : g + 1, :] = src8[0:1, g * LANES : (g + 1) * LANES]

    def to_lanes(value, dst8):
        for g in range(CHUNKS):
            dst8[:, g * LANES : (g + 1) * LANES] = jnp.broadcast_to(value[g : g + 1, :], (8, LANES))

    to_dense(peak8, rowpart.at[0])
    pl.semaphore_wait(barrier, NY * NZ - 1 + NX - 1 + 1)

    def x_exchange(t):
        xbuf[t, x] = rowpart[t]

        def one(dx):
            return copy(rowpart.at[t], xbuf.at[t, x], x_s.at[t, dx - 1], x_r.at[t, dx - 1], dev(dx=dx))

        for dx in (2, 1, 3):
            one(dx).start()
        for dx in (1, 3, 2):
            one(dx).wait_recv()
        for dx in (1, 3, 2):
            one(dx).wait_send()

    x_exchange(0)
    peak = jnp.maximum(jnp.maximum(xbuf[0, 0], xbuf[0, 1]), jnp.maximum(xbuf[0, 2], xbuf[0, 3]))
    factor[...] = jnp.exp2(rowpart[0] - peak)
    to_lanes(factor[...], row_b)

    ones = jnp.ones((8, LANES), jnp.float32)

    def lane_sums(h, t):
        for g in range(NZ):
            at = pl.ds(pl.multiple_of(h * HALF + g * LANES, LANES), LANES)
            s = lax.dot_general(
                ones, acc[at, :], NT, preferred_element_type=jnp.float32, precision=lax.Precision.HIGHEST
            )
            dense[t, h, g : g + 1, :] = s[0:1, :]

    def col_pass(h):
        r = [row_b[:, k * LANES : (k + 1) * LANES] for k in range(CHUNKS)]

        def body(q, carry):
            at = pl.ds(pl.multiple_of(h * HALF + q * 8, 8), 8)
            terms = [expo[at, k * LANES : (k + 1) * LANES] * r[k] for k in range(CHUNKS)]
            while len(terms) > 1:
                terms = [a + b for a, b in zip(terms[::2], terms[1::2])]
            acc[at, :] = terms[0]
            return carry

        lax.fori_loop(0, HALF // 8, body, 0, unroll=4)

    def row_pass(h, carry):
        def body(q, carry):
            at = pl.ds(pl.multiple_of(h * HALF + q * 8, 8), 8)
            c = col_b[at, :]
            return tuple(carry[k] + expo[at, k * LANES : (k + 1) * LANES] * c for k in range(CHUNKS))

        return lax.fori_loop(0, HALF // 8, body, carry, unroll=4)

    def pre_copy(t):
        return copy(dense.at[t, other], pre.at[t], pre_s.at[t], pre_r.at[t], dev(flip=True))

    def post_copy(t):
        return copy(total.at[t, core], total.at[t, core], post_s.at[t], post_r.at[t], dev(flip=True))

    def col_copy(t, i, dy):
        k = i * NY + dy
        return copy(own.at[t], colbuf.at[t, k], col_s.at[t, k], col_r.at[t, k], dev(dy=dy, dz=far_first(i)))

    def each_peer(act):
        def body(i, carry):
            for dy in (2, 1, 3):
                act(i, dy)

            @pl.when(i < NZ - 1)
            def _():
                act(i, 0)

            return carry

        lax.fori_loop(0, NZ, body, 0)

    def col_send(t):
        pre_copy(t).wait_recv()
        own[t] = dense[t, core] + pre[t]
        each_peer(lambda i, dy: col_copy(t, i, dy).start())

    def col_finish(t):
        each_peer(lambda i, dy: col_copy(t, i, dy).wait_recv())
        terms = [colbuf[t, k] for k in range(NY * NZ) if k != NY * (NZ - 1)] + [own[t]]
        while len(terms) > 1:
            terms = [a + b for a, b in zip(terms[::2], terms[1::2])]
        total[t, core] = terms[0]
        each_peer(lambda i, dy: col_copy(t, i, dy).wait_send())
        pre_copy(t).wait_send()

    def scale_half(t, h):
        scale = ratio / jnp.maximum(total[t, h], 1.0)
        for g in range(NZ):
            at = pl.ds(pl.multiple_of(h * HALF + g * LANES, LANES), LANES)
            col_b[at, :] = jnp.broadcast_to(scale[g : g + 1, :], (LANES, LANES)).T

    def one_round(t, carry):
        col_pass(other)
        lane_sums(other, t)
        pre_copy(t).start()
        col_pass(core)
        lane_sums(core, t)
        col_send(t)
        col_finish(t)
        post_copy(t).start()
        scale_half(t, core)
        mass = row_pass(core, tuple(jnp.zeros((8, LANES), jnp.float32) for _ in range(CHUNKS)))
        post_copy(t).wait_recv()
        scale_half(t, other)
        mass = row_pass(other, mass)
        for g in range(CHUNKS):
            rowpart[t + 1, g : g + 1, :] = jnp.sum(mass[g], axis=0, keepdims=True)
        rowpart[t + 1] = rowpart[t + 1] * factor[...]
        x_exchange(t + 1)
        row_mass = (xbuf[t + 1, 0] + xbuf[t + 1, 1]) + (xbuf[t + 1, 2] + xbuf[t + 1, 3])
        log_ref[...] = -jnp.log(row_mass)
        to_lanes(factor[...] / row_mass, row_b)
        post_copy(t).wait_send()
        return carry

    lax.fori_loop(0, ITERS, one_round, 0)

    def core_copy(i):
        return copy(numer.at[i, 1], corebuf.at[i], core_s.at[i], core_r.at[i], dev(flip=True))

    def y_copy(i, dy):
        at = pl.ds(pl.multiple_of(lax.rem(y + dy, NY) * SHARD, SHARD), SHARD)
        return copy(numer.at[i, 0, at], ybuf.at[i, dy - 1], y_s.at[i, dy - 1], y_r.at[i, dy - 1], dev(dy=dy))

    def z_copy(i):
        return copy(zsrc.at[i], zbuf.at[i], z_s.at[i], z_r.at[i], dev(dz=far_first(i)))

    def group(i, carry):
        @pl.when(i < NZ)
        def _():
            to = lax.rem(z + far_first(i), NZ)
            for n, h in enumerate((core, other)):
                base = h * HALF + to * GROUP

                def body(q, carry):
                    at = pl.ds(pl.multiple_of(base + q * 16, 16), 16)
                    c = col_b[at, :]
                    terms = []
                    for k in range(CHUNKS):
                        lanes = slice(k * LANES, (k + 1) * LANES)
                        r = row_b[:, lanes]
                        w = expo[at, lanes] * jnp.concatenate([r, r], axis=0) * c
                        low[pl.ds(pl.multiple_of(n * GROUP + q * 16, 16), 16), lanes] = w.astype(jnp.bfloat16)
                        terms.append(w)
                    while len(terms) > 1:
                        terms = [a + b for a, b in zip(terms[::2], terms[1::2])]
                    acc[at, :] = terms[0]
                    return carry

                lax.fori_loop(0, GROUP // 16, body, 0, unroll=2)
            both = jnp.dot(low[...], p_ref[...], preferred_element_type=jnp.float32)
            numer[i, 0] = both[:GROUP]
            numer[i, 1] = both[GROUP:]
            core_copy(i).start()

        @pl.when(i >= 2)
        def _():
            j = i - 2
            core_copy(j).wait_recv()
            numer[j, 0] = numer[j, 0] + corebuf[j]
            for dy in (2, 1, 3):
                y_copy(j, dy).start()

        return carry

    lax.fori_loop(0, NZ + 2, group, 0)

    lane_sums(other, ITERS)
    pre_copy(ITERS).start()
    lane_sums(core, ITERS)
    col_send(ITERS)

    def z_step(i, carry):
        for dy in (1, 3, 2):
            y_copy(i, dy).wait_recv()
        at = pl.ds(pl.multiple_of(y * SHARD, SHARD), SHARD)
        zsrc[i] = (numer[i, 0, at] + ybuf[i, 0]) + (ybuf[i, 1] + ybuf[i, 2])

        @pl.when(i < NZ - 1)
        def _():
            z_copy(i).start()

        return carry

    lax.fori_loop(0, NZ, z_step, 0)

    col_finish(ITERS)
    weight = jnp.maximum(total[ITERS, core, pl.ds(z, 1), :], 1.0)
    norm_b[0:LANES, :] = jnp.broadcast_to(weight, (LANES, LANES)).T

    for i in range(NZ - 1):
        z_copy(i).wait_recv()
    numer_sum = zsrc[NZ - 1]
    for i in range(NZ - 1):
        numer_sum = numer_sum + zbuf[i]
    w = norm_b[pl.ds(pl.multiple_of(y * SHARD, SHARD), SHARD), :]

    def piece(zz, yy):
        return new_ref.at[pl.ds(pl.multiple_of(core * HALF + zz * GROUP + yy * SHARD, SHARD), SHARD)]

    mine = piece(z, y)
    mine[...] = numer_sum / jnp.concatenate([w, w], axis=1)

    def agz_copy(i):
        return copy(mine, mine, agz_s.at[i], agz_r.at[i], dev(dz=far_first(i)))

    def agy_copy(i, dy):
        part = piece(lax.rem(z + NZ - far_first(i), NZ), y)
        return copy(part, part, agy_s.at[i, dy - 1], agy_r.at[i, dy - 1], dev(dy=dy))

    def agc_copy(i):
        zz = lax.rem(z + NZ - far_first(i), NZ)
        part = new_ref.at[pl.ds(pl.multiple_of(core * HALF + zz * GROUP, GROUP), GROUP)]
        return copy(part, part, agc_s.at[i], agc_r.at[i], dev(flip=True))

    def gather_z(i, carry):
        agz_copy(i).start()
        return carry

    lax.fori_loop(0, NZ - 1, gather_z, 0)

    def gather_y(n, carry):
        i = NZ - 1 - n

        @pl.when(n > 0)
        def _():
            agz_copy(i).wait_recv()

        for dy in (2, 1, 3):
            agy_copy(i, dy).start()
        return carry

    lax.fori_loop(0, NZ, gather_y, 0)

    def gather_core(n, carry):
        i = NZ - 1 - n
        for dy in (1, 3, 2):
            agy_copy(i, dy).wait_recv()
        agc_copy(i).start()
        return carry

    lax.fori_loop(0, NZ, gather_core, 0)

    def finish(i, carry):
        agc_copy(i).wait_recv()
        agc_copy(i).wait_send()
        core_copy(i).wait_send()
        for dy in (1, 2, 3):
            y_copy(i, dy).wait_send()
            agy_copy(i, dy).wait_send()

        @pl.when(i < NZ - 1)
        def _():
            z_copy(i).wait_send()
            agz_copy(i).wait_send()

        return carry

    lax.fori_loop(0, NZ, finish, 0)


def local(patients, centroids):
    ratio = float(R * NY * NZ * 2) / float(K * NX)
    f32 = jnp.float32
    T = ITERS + 1
    dma = pltpu.SemaphoreType.DMA
    vm = pltpu.VMEM
    new, log = pl.pallas_call(
        functools.partial(kernel, ratio),
        out_shape=(jax.ShapeDtypeStruct((K, D), f32), jax.ShapeDtypeStruct((CHUNKS, LANES), f32)),
        in_specs=[pl.BlockSpec(memory_space=pltpu.VMEM)] * 2,
        out_specs=[pl.BlockSpec(memory_space=pltpu.VMEM)] * 2,
        scratch_shapes=[
            vm((K, R), f32), vm((K, LANES), f32), vm((8, R), f32), vm((K, LANES), f32), vm((K, LANES), f32),
            vm((8, R), f32), vm((CHUNKS, LANES), f32),
            vm((T, 2, NZ, LANES), f32), vm((T, NZ, LANES), f32), vm((T, NZ, LANES), f32),
            vm((T, NY * NZ, NZ, LANES), f32), vm((T, 2, NZ, LANES), f32),
            vm((T, CHUNKS, LANES), f32), vm((T, NX, CHUNKS, LANES), f32),
            vm((2 * GROUP, R), jnp.bfloat16), vm((NZ, 2, GROUP, D), f32), vm((NZ, GROUP, D), f32),
            vm((NZ, NY - 1, SHARD, D), f32), vm((NZ, SHARD, D), f32), vm((NZ - 1, SHARD, D), f32),
            dma((T,)), dma((T,)), dma((T, NY * NZ)), dma((T, NY * NZ)), dma((T,)), dma((T,)),
            dma((T, NX - 1)), dma((T, NX - 1)),
            dma((NZ,)), dma((NZ,)), dma((NZ, NY - 1)), dma((NZ, NY - 1)), dma((NZ,)), dma((NZ,)),
            dma((NZ,)), dma((NZ,)), dma((NZ, NY - 1)), dma((NZ, NY - 1)), dma((NZ,)), dma((NZ,)),
        ],
        compiler_params=pltpu.CompilerParams(
            collective_id=0, has_side_effects=True, vmem_limit_bytes=48 << 20
        ),
    )(patients, centroids)
    return new, log.reshape(R)


def solution(mesh):
    return jax.shard_map(
        local,
        mesh=mesh,
        in_specs=(P("rows", None), P("cents", None)),
        out_specs=(P("cents", None), P("rows")),
        check_vma=False,
    )
```

time: 693 us -> 120 us (0.17)
  blocking collectives: 547 us -> 0 us
  Pallas kernels: 0 us -> 115 us
  other arithmetic: 64.6 us -> 0 us
  waiting for transfers between devices: 46.1 us -> 0 us
  matrix products: 19.4 us -> 0 us
  between operations: 14.2 us -> 0.65 us
    psum x7 -> x0, blocking collectives: 538 us -> none  [the longest x3 390 us: local(): column_mass = lax.psum(jnp.sum(expo * row_scale[:, None], axis=0), 'rows')]
    pallas_call x0 -> x1, Pallas kernels: none -> 115 us  [local(): pl.pallas_call(functools.partial(kernel, ratio), out_shape=(jax.ShapeDtyp...]
    reduce_sum x8 -> x0, other arithmetic: 60.7 us -> none  [the longest x3 25.5 us: local(): row_mass = lax.psum(jnp.sum(expo * col_scale[None, :], axis=1), 'cents')]
    psum x1 -> x0, waiting for transfers between devices: 46.1 us -> none  [local(): numer, weight = lax.psum((numer_local, weight_local), 'rows')]
    dot_general x2 -> x0, matrix products: 19.4 us -> none  [the longest x1 11.1 us: local(): lax.dot_general(assign_low, patients, (((0,), (0,)), ((), ())), preferred...]
    pmax x1 -> x0, blocking collectives: 9.38 us -> none  [local(): peak = lax.pmax(jnp.max(logits, axis=1), 'cents')]
  transfers between devices with their start and end apart: 1 -> 0, of which waited for: 1 -> 0; matrix products, arithmetic and copies ran while one was open for 1% -> 0% of each run, Pallas kernels for 0% -> 0%
where the time goes in v1:
time: 120 us
  Pallas kernels  115 us (96%)
  local copies, waits for them, and re-layouts  4.36 us (4%)
    pallas_call x1, Pallas kernels, local(): pl.pallas_call(functools.partial(kernel, ratio), out_shape=(jax.ShapeDtyp...  115 us
    unnamed x6, local copies, waits for them, and re-layouts  4.36 us

profile of v1, /device:TPU:1, one launch (start us, length us, event | category | flops | bytes accessed | tf_op | source)
XLA Modules:
  0.0 120.0 jit_solution(14686178280870233828)
XLA Ops:
  0.6 0.0 copy-start
  0.6 1.2 %copy-done = bf16[2048,256]{1,0:T(8,128)(2,1)S(1)} copy-done((bf16[2048,256]{1,0:T(8,128)(2,1)S(1)}, bf16[2048,256]{1,0:T(8,128)(2,1)}, u32[]{:S(2)}) %copy-start) | copy-done | bytes 1048600
  1.9 0.0 copy-start.1
  1.9 1.2 %copy-done.1 = bf16[2048,256]{1,0:T(8,128)(2,1)S(1)} copy-done((bf16[2048,256]{1,0:T(8,128)(2,1)S(1)}, bf16[2048,256]{1,0:T(8,128)(2,1)}, u32[]{:S(2)}) %copy-start.1) | copy-done | bytes 1048600
  3.1 115.0 %shard_map.41 = (f32[2048,256]{1,0:T(8,128)S(1)}, f32[16,128]{1,0:T(8,128)S(1)}) custom-call(bf16[2048,256]{1,0:T(8,128)(2,1)S(1)} %copy-done, bf16[2048,256]{1,0:T(8,128)(2,1)S(1)} %copy-done.1), custom_call_target="tpu_custom_call" | custom-call | tf_op jit(solution)/shard_map/pallas_call | solution.py:394
  118.1 1.3 %copy.6 = f32[2048,256]{1,0:T(8,128)} copy(f32[2048,256]{1,0:T(8,128)S(1)} %get-tuple-element.8) | data formatting | bytes 4194304
  119.4 0.6 copy.7
Async XLA Ops:
  0.6 1.2 %copy-start = (bf16[2048,256]{1,0:T(8,128)(2,1)S(1)}, bf16[2048,256]{1,0:T(8,128)(2,1)}, u32[]{:S(2)}) copy-start(bf16[2048,256]{1,0:T(8,128)(2,1)} %p_ref.1) | copy-start | bytes 3145732
  1.9 1.2 %copy-start.1 = (bf16[2048,256]{1,0:T(8,128)(2,1)S(1)}, bf16[2048,256]{1,0:T(8,128)(2,1)}, u32[]{:S(2)}) copy-start(bf16[2048,256]{1,0:T(8,128)(2,1)} %c_ref.1) | copy-start | bytes 3145732

commit v2 on v1

--- a/solution.py
+++ b/solution.py
@@ -22,6 +22,8 @@
 LANES = 128
 CHUNKS = R // LANES
 MESH = pl.DeviceIdType.MESH
+Y_LAG = 4
+G_LAG = 4
 NT = (((1,), (1,)), ((), ()))
 
 
@@ -31,12 +33,12 @@
 
 
 def kernel(
-    ratio, p_ref, c_ref, new_ref, log_ref,
+    ratio, p_hbm, c_hbm, new_ref, log_ref, p_ref, c_ref, t_even, t_odd, in_s,
     expo, col_b, row_b, acc, norm_b, peak8, factor,
     dense, pre, own, colbuf, total, rowpart, xbuf,
-    low, numer, corebuf, ybuf, zsrc, zbuf,
+    low, numer, corebuf, relaybuf, ybuf, zsrc, zbuf,
     pre_s, pre_r, col_s, col_r, post_s, post_r, x_s, x_r,
-    core_s, core_r, y_s, y_r, z_s, z_r, agz_s, agz_r, agy_s, agy_r, agc_s, agc_r,
+    core_s, core_r, relay_s, relay_r, y_s, y_r, z_s, z_r, agz_s, agz_r, agy_s, agy_r, agf_s, agf_r, agc_s, agc_r,
 ):
     x = lax.axis_index("cents")
     rows = lax.axis_index("rows")
@@ -56,6 +58,11 @@
             src_ref=src, dst_ref=dst, send_sem=send, recv_sem=recv, device_id=to, device_id_type=MESH
         )
 
+    fetch_c = pltpu.make_async_copy(c_hbm, c_ref, in_s.at[0])
+    fetch_p = pltpu.make_async_copy(p_hbm, p_ref, in_s.at[1])
+    fetch_c.start()
+    fetch_p.start()
+
     barrier = pltpu.get_barrier_semaphore()
 
     def greet(i, carry):
@@ -82,35 +89,48 @@
         )
         return carry
 
+    fetch_c.wait()
     lax.fori_loop(0, K // 256, norms, 0)
-
-    def scores(b, carry):
-        lanes = pl.ds(pl.multiple_of(b * 256, 256), 256)
-        block = p_ref[lanes, :]
-
-        def part(q, top):
-            at = pl.ds(pl.multiple_of(q * 512, 512), 512)
-            s = lax.dot_general(c_ref[at, :], block, NT, preferred_element_type=jnp.float32)
-            bias = norm_b[at, :]
-            t = s * (2.0 * LOG2E / TAU) - jnp.concatenate([bias, bias], axis=1)
-            expo[at, lanes] = t
-            return jnp.maximum(top, jnp.max(t.reshape(64, 8, 256), axis=0))
-
-        top = lax.fori_loop(0, K // 512, part, jnp.full((8, 256), -jnp.inf, jnp.float32))
-        top = jnp.max(top, axis=0, keepdims=True)
-        peak8[:, lanes] = jnp.broadcast_to(top, (8, 256))
-        return carry
-
-    lax.fori_loop(0, R // 256, scores, 0)
-
-    def exps(q, carry):
-        at = pl.ds(pl.multiple_of(q * 8, 8), 8)
-        for k in range(CHUNKS):
-            lanes = slice(k * LANES, (k + 1) * LANES)
-            expo[at, lanes] = jnp.exp2(expo[at, lanes] - peak8[:, lanes])
-        return carry
-
-    lax.fori_loop(0, K // 8, exps, 0, unroll=4)
+    fetch_p.wait()
+
+    def block_lanes(b):
+        return pl.ds(pl.multiple_of(b * 256, 256), 256)
+
+    def score_part(q, b, buf):
+        at = slice(q * 512, (q + 1) * 512)
+        s = lax.dot_general(c_ref[at, :], p_ref[block_lanes(b), :], NT, preferred_element_type=jnp.float32)
+        bias = norm_b[at, :]
+        t = s * (2.0 * LOG2E / TAU) - jnp.concatenate([bias, bias], axis=1)
+        buf[at, :] = t
+        return jnp.max(t.reshape(64, 8, 256), axis=0)
+
+    def exp_part(q, b, buf, top):
+        at = slice(q * 512, (q + 1) * 512)
+        expo[at, block_lanes(b)] = jnp.exp2(buf[at, :] - top)
+
+    def set_peak(b, tops):
+        top = jnp.max(jnp.maximum(jnp.maximum(tops[0], tops[1]), jnp.maximum(tops[2], tops[3])), axis=0, keepdims=True)
+        peak8[:, block_lanes(b)] = jnp.broadcast_to(top, (8, 256))
+
+    def step(b, buf, last):
+        top = peak8[0:1, block_lanes(b - 1)]
+        tops = []
+        for q in range(4):
+            tops.append(score_part(q, b, buf))
+            exp_part(q, b - 1, last, top)
+        set_peak(b, tops)
+
+    set_peak(0, [score_part(q, 0, t_even) for q in range(4)])
+
+    def pair(m, carry):
+        step(2 * m + 1, t_odd, t_even)
+        step(2 * m + 2, t_even, t_odd)
+        return carry
+
+    lax.fori_loop(0, R // 512 - 1, pair, 0)
+    step(R // 256 - 1, t_odd, t_even)
+    for q in range(4):
+        exp_part(q, R // 256 - 1, t_odd, peak8[0:1, R - 256 :])
 
     def to_dense(src8, dst):
         for g in range(CHUNKS):
@@ -244,9 +264,17 @@
     def core_copy(i):
         return copy(numer.at[i, 1], corebuf.at[i], core_s.at[i], core_r.at[i], dev(flip=True))
 
-    def y_copy(i, dy):
-        at = pl.ds(pl.multiple_of(lax.rem(y + dy, NY) * SHARD, SHARD), SHARD)
-        return copy(numer.at[i, 0, at], ybuf.at[i, dy - 1], y_s.at[i, dy - 1], y_r.at[i, dy - 1], dev(dy=dy))
+    near, back = 1 + 2 * core, 3 - 2 * core
+
+    def part_of(i, dy):
+        return numer.at[i, 0, pl.ds(pl.multiple_of(lax.rem(y + dy, NY) * SHARD, SHARD), SHARD)]
+
+    def relay_copy(i):
+        return copy(part_of(i, 2), relaybuf.at[i], relay_s.at[i], relay_r.at[i], dev(dy=near))
+
+    def y_copy(i, n):
+        dy = (near, back)[n]
+        return copy(part_of(i, dy), ybuf.at[i, n], y_s.at[i, n], y_r.at[i, n], dev(dy=dy))
 
     def z_copy(i):
         return copy(zsrc.at[i], zbuf.at[i], z_s.at[i], z_r.at[i], dev(dz=far_first(i)))
@@ -284,8 +312,8 @@
             j = i - 2
             core_copy(j).wait_recv()
             numer[j, 0] = numer[j, 0] + corebuf[j]
-            for dy in (2, 1, 3):
-                y_copy(j, dy).start()
+            relay_copy(j).start()
+            y_copy(j, 1).start()
 
         return carry
 
@@ -296,19 +324,33 @@
     lane_sums(core, ITERS)
     col_send(ITERS)
 
-    def z_step(i, carry):
-        for dy in (1, 3, 2):
-            y_copy(i, dy).wait_recv()
-        at = pl.ds(pl.multiple_of(y * SHARD, SHARD), SHARD)
-        zsrc[i] = (numer[i, 0, at] + ybuf[i, 0]) + (ybuf[i, 1] + ybuf[i, 2])
+    def relay(i):
+        relay_copy(i).wait_recv()
+        part = part_of(i, near)
+        part[...] = part[...] + relaybuf[i]
+        y_copy(i, 0).start()
+
+    def z_step(i):
+        y_copy(i, 1).wait_recv()
+        y_copy(i, 0).wait_recv()
+        zsrc[i] = part_of(i, 0)[...] + (ybuf[i, 0] + ybuf[i, 1])
 
         @pl.when(i < NZ - 1)
         def _():
             z_copy(i).start()
 
-        return carry
-
-    lax.fori_loop(0, NZ, z_step, 0)
+    def scatter(n, carry):
+        @pl.when(n < NZ)
+        def _():
+            relay(n)
+
+        @pl.when(n >= Y_LAG)
+        def _():
+            z_step(n - Y_LAG)
+
+        return carry
+
+    lax.fori_loop(0, NZ + Y_LAG, scatter, 0)
 
     col_finish(ITERS)
     weight = jnp.maximum(total[ITERS, core, pl.ds(z, 1), :], 1.0)
@@ -330,12 +372,19 @@
     def agz_copy(i):
         return copy(mine, mine, agz_s.at[i], agz_r.at[i], dev(dz=far_first(i)))
 
-    def agy_copy(i, dy):
-        part = piece(lax.rem(z + NZ - far_first(i), NZ), y)
-        return copy(part, part, agy_s.at[i, dy - 1], agy_r.at[i, dy - 1], dev(dy=dy))
+    def from_z(i):
+        return lax.rem(z + NZ - far_first(i), NZ)
+
+    def agy_copy(i, n):
+        part = piece(from_z(i), y)
+        return copy(part, part, agy_s.at[i, n], agy_r.at[i, n], dev(dy=(near, back)[n]))
+
+    def agf_copy(i):
+        part = piece(from_z(i), lax.rem(y + back, NY))
+        return copy(part, part, agf_s.at[i], agf_r.at[i], dev(dy=near))
 
     def agc_copy(i):
-        zz = lax.rem(z + NZ - far_first(i), NZ)
+        zz = from_z(i)
         part = new_ref.at[pl.ds(pl.multiple_of(core * HALF + zz * GROUP, GROUP), GROUP)]
         return copy(part, part, agc_s.at[i], agc_r.at[i], dev(flip=True))
 
@@ -345,35 +394,44 @@
 
     lax.fori_loop(0, NZ - 1, gather_z, 0)
 
-    def gather_y(n, carry):
-        i = NZ - 1 - n
-
-        @pl.when(n > 0)
-        def _():
-            agz_copy(i).wait_recv()
-
-        for dy in (2, 1, 3):
-            agy_copy(i, dy).start()
-        return carry
-
-    lax.fori_loop(0, NZ, gather_y, 0)
-
-    def gather_core(n, carry):
-        i = NZ - 1 - n
-        for dy in (1, 3, 2):
-            agy_copy(i, dy).wait_recv()
-        agc_copy(i).start()
-        return carry
-
-    lax.fori_loop(0, NZ, gather_core, 0)
+    def gather(n, carry):
+        @pl.when(n < NZ)
+        def _():
+            i = NZ - 1 - n
+
+            @pl.when(n > 0)
+            def _():
+                agz_copy(i).wait_recv()
+
+            agy_copy(i, 0).start()
+            agy_copy(i, 1).start()
+
+        @pl.when((n >= G_LAG) & (n < NZ + G_LAG))
+        def _():
+            i = NZ - 1 - (n - G_LAG)
+            agy_copy(i, 0).wait_recv()
+            agf_copy(i).start()
+
+        @pl.when(n >= 2 * G_LAG)
+        def _():
+            i = NZ - 1 - (n - 2 * G_LAG)
+            agy_copy(i, 1).wait_recv()
+            agf_copy(i).wait_recv()
+            agc_copy(i).start()
+
+        return carry
+
+    lax.fori_loop(0, NZ + 2 * G_LAG, gather, 0)
 
     def finish(i, carry):
         agc_copy(i).wait_recv()
         agc_copy(i).wait_send()
         core_copy(i).wait_send()
-        for dy in (1, 2, 3):
-            y_copy(i, dy).wait_send()
-            agy_copy(i, dy).wait_send()
+        relay_copy(i).wait_send()
+        agf_copy(i).wait_send()
+        for n in range(2):
+            y_copy(i, n).wait_send()
+            agy_copy(i, n).wait_send()
 
         @pl.when(i < NZ - 1)
         def _():
@@ -394,20 +452,21 @@
     new, log = pl.pallas_call(
         functools.partial(kernel, ratio),
         out_shape=(jax.ShapeDtypeStruct((K, D), f32), jax.ShapeDtypeStruct((CHUNKS, LANES), f32)),
-        in_specs=[pl.BlockSpec(memory_space=pltpu.VMEM)] * 2,
+        in_specs=[pl.BlockSpec(memory_space=pltpu.HBM)] * 2,
         out_specs=[pl.BlockSpec(memory_space=pltpu.VMEM)] * 2,
         scratch_shapes=[
+            vm((R, D), jnp.bfloat16), vm((K, D), jnp.bfloat16), vm((K, 256), f32), vm((K, 256), f32), dma((2,)),
             vm((K, R), f32), vm((K, LANES), f32), vm((8, R), f32), vm((K, LANES), f32), vm((K, LANES), f32),
             vm((8, R), f32), vm((CHUNKS, LANES), f32),
             vm((T, 2, NZ, LANES), f32), vm((T, NZ, LANES), f32), vm((T, NZ, LANES), f32),
             vm((T, NY * NZ, NZ, LANES), f32), vm((T, 2, NZ, LANES), f32),
             vm((T, CHUNKS, LANES), f32), vm((T, NX, CHUNKS, LANES), f32),
             vm((2 * GROUP, R), jnp.bfloat16), vm((NZ, 2, GROUP, D), f32), vm((NZ, GROUP, D), f32),
-            vm((NZ, NY - 1, SHARD, D), f32), vm((NZ, SHARD, D), f32), vm((NZ - 1, SHARD, D), f32),
+            vm((NZ, SHARD, D), f32), vm((NZ, 2, SHARD, D), f32), vm((NZ, SHARD, D), f32), vm((NZ - 1, SHARD, D), f32),
             dma((T,)), dma((T,)), dma((T, NY * NZ)), dma((T, NY * NZ)), dma((T,)), dma((T,)),
             dma((T, NX - 1)), dma((T, NX - 1)),
-            dma((NZ,)), dma((NZ,)), dma((NZ, NY - 1)), dma((NZ, NY - 1)), dma((NZ,)), dma((NZ,)),
-            dma((NZ,)), dma((NZ,)), dma((NZ, NY - 1)), dma((NZ, NY - 1)), dma((NZ,)), dma((NZ,)),
+            dma((NZ,)), dma((NZ,)), dma((NZ,)), dma((NZ,)), dma((NZ, 2)), dma((NZ, 2)), dma((NZ,)), dma((NZ,)),
+            dma((NZ,)), dma((NZ,)), dma((NZ, 2)), dma((NZ, 2)), dma((NZ,)), dma((NZ,)), dma((NZ,)), dma((NZ,)),
         ],
         compiler_params=pltpu.CompilerParams(
             collective_id=0, has_side_effects=True, vmem_limit_bytes=48 << 20

time: 120 us -> 114 us (0.950)
  Pallas kernels: 115 us -> 109 us
    pallas_call x1, Pallas kernels: 115 us -> 109 us  [local(): pl.pallas_call(functools.partial(kernel, ratio), out_shape=(jax.ShapeDtyp...]
where the time goes in v2:
time: 114 us
  Pallas kernels  109 us (96%)
  local copies, waits for them, and re-layouts  4.36 us (4%)
    pallas_call x1, Pallas kernels, local(): pl.pallas_call(functools.partial(kernel, ratio), out_shape=(jax.ShapeDtyp...  109 us
    unnamed x6, local copies, waits for them, and re-layouts  4.36 us

profile of v2, /device:TPU:1, one launch (start us, length us, event | category | flops | bytes accessed | tf_op | source)
XLA Modules:
  0.0 113.8 jit_solution(15823301604221427417)
XLA Ops:
  0.6 0.0 copy-start
  0.6 1.2 %copy-done = bf16[2048,256]{1,0:T(8,128)(2,1)S(1)} copy-done((bf16[2048,256]{1,0:T(8,128)(2,1)S(1)}, bf16[2048,256]{1,0:T(8,128)(2,1)}, u32[]{:S(2)}) %copy-start) | copy-done | bytes 1048600
  1.9 0.0 copy-start.1
  1.9 1.2 %copy-done.1 = bf16[2048,256]{1,0:T(8,128)(2,1)S(1)} copy-done((bf16[2048,256]{1,0:T(8,128)(2,1)S(1)}, bf16[2048,256]{1,0:T(8,128)(2,1)}, u32[]{:S(2)}) %copy-start.1) | copy-done | bytes 1048600
  3.1 108.8 %shard_map.41 = (f32[2048,256]{1,0:T(8,128)S(1)}, f32[16,128]{1,0:T(8,128)S(1)}) custom-call(bf16[2048,256]{1,0:T(8,128)(2,1)S(1)} %copy-done, bf16[2048,256]{1,0:T(8,128)(2,1)S(1)} %copy-done.1), custom_call_target="tpu_custom_call" | custom-call | tf_op jit(solution)/shard_map/pallas_call | solution.py:452
  111.9 1.3 %copy.6 = f32[2048,256]{1,0:T(8,128)} copy(f32[2048,256]{1,0:T(8,128)S(1)} %get-tuple-element.8) | data formatting | bytes 4194304
  113.2 0.6 copy.7
Async XLA Ops:
  0.6 1.2 %copy-start = (bf16[2048,256]{1,0:T(8,128)(2,1)S(1)}, bf16[2048,256]{1,0:T(8,128)(2,1)}, u32[]{:S(2)}) copy-start(bf16[2048,256]{1,0:T(8,128)(2,1)} %p_hbm.1) | copy-start | bytes 3145732
  1.9 1.2 %copy-start.1 = (bf16[2048,256]{1,0:T(8,128)(2,1)S(1)}, bf16[2048,256]{1,0:T(8,128)(2,1)}, u32[]{:S(2)}) copy-start(bf16[2048,256]{1,0:T(8,128)(2,1)} %c_hbm.1) | copy-start | bytes 3145732

commit v3 on v2

--- a/solution.py
+++ b/solution.py
@@ -22,7 +22,7 @@
 LANES = 128
 CHUNKS = R // LANES
 MESH = pl.DeviceIdType.MESH
-Y_LAG = 4
+Y_LAG = 7
 G_LAG = 4
 NT = (((1,), (1,)), ((), ()))
 
@@ -36,9 +36,9 @@
     ratio, p_hbm, c_hbm, new_ref, log_ref, p_ref, c_ref, t_even, t_odd, in_s,
     expo, col_b, row_b, acc, norm_b, peak8, factor,
     dense, pre, own, colbuf, total, rowpart, xbuf,
-    low, numer, corebuf, relaybuf, ybuf, zsrc, zbuf,
+    low, numer, corebuf, ybuf, zsrc, zbuf,
     pre_s, pre_r, col_s, col_r, post_s, post_r, x_s, x_r,
-    core_s, core_r, relay_s, relay_r, y_s, y_r, z_s, z_r, agz_s, agz_r, agy_s, agy_r, agf_s, agf_r, agc_s, agc_r,
+    core_s, core_r, y_s, y_r, z_s, z_r, agz_s, agz_r, agy_s, agy_r, agc_s, agc_r,
 ):
     x = lax.axis_index("cents")
     rows = lax.axis_index("rows")
@@ -264,20 +264,23 @@
     def core_copy(i):
         return copy(numer.at[i, 1], corebuf.at[i], core_s.at[i], core_r.at[i], dev(flip=True))
 
-    near, back = 1 + 2 * core, 3 - 2 * core
-
     def part_of(i, dy):
         return numer.at[i, 0, pl.ds(pl.multiple_of(lax.rem(y + dy, NY) * SHARD, SHARD), SHARD)]
 
-    def relay_copy(i):
-        return copy(part_of(i, 2), relaybuf.at[i], relay_s.at[i], relay_r.at[i], dev(dy=near))
-
-    def y_copy(i, n):
-        dy = (near, back)[n]
-        return copy(part_of(i, dy), ybuf.at[i, n], y_s.at[i, n], y_r.at[i, n], dev(dy=dy))
+    def y_copy(i, dy):
+        return copy(part_of(i, dy), ybuf.at[i, dy - 1], y_s.at[i, dy - 1], y_r.at[i, dy - 1], dev(dy=dy))
 
     def z_copy(i):
         return copy(zsrc.at[i], zbuf.at[i], z_s.at[i], z_r.at[i], dev(dz=far_first(i)))
+
+    def z_step(i):
+        for dy in (1, 3, 2):
+            y_copy(i, dy).wait_recv()
+        zsrc[i] = (part_of(i, 0)[...] + ybuf[i, 0]) + (ybuf[i, 1] + ybuf[i, 2])
+
+        @pl.when(i < NZ - 1)
+        def _():
+            z_copy(i).start()
 
     def group(i, carry):
         @pl.when(i < NZ)
@@ -312,8 +315,12 @@
             j = i - 2
             core_copy(j).wait_recv()
             numer[j, 0] = numer[j, 0] + corebuf[j]
-            relay_copy(j).start()
-            y_copy(j, 1).start()
+            for dy in (2, 1, 3):
+                y_copy(j, dy).start()
+
+        @pl.when(i >= Y_LAG)
+        def _():
+            z_step(i - Y_LAG)
 
         return carry
 
@@ -324,33 +331,11 @@
     lane_sums(core, ITERS)
     col_send(ITERS)
 
-    def relay(i):
-        relay_copy(i).wait_recv()
-        part = part_of(i, near)
-        part[...] = part[...] + relaybuf[i]
-        y_copy(i, 0).start()
-
-    def z_step(i):
-        y_copy(i, 1).wait_recv()
-        y_copy(i, 0).wait_recv()
-        zsrc[i] = part_of(i, 0)[...] + (ybuf[i, 0] + ybuf[i, 1])
-
-        @pl.when(i < NZ - 1)
-        def _():
-            z_copy(i).start()
-
-    def scatter(n, carry):
-        @pl.when(n < NZ)
-        def _():
-            relay(n)
-
-        @pl.when(n >= Y_LAG)
-        def _():
-            z_step(n - Y_LAG)
-
-        return carry
-
-    lax.fori_loop(0, NZ + Y_LAG, scatter, 0)
+    def scatter(i, carry):
+        z_step(i)
+        return carry
+
+    lax.fori_loop(NZ + 2 - Y_LAG, NZ, scatter, 0)
 
     col_finish(ITERS)
     weight = jnp.maximum(total[ITERS, core, pl.ds(z, 1), :], 1.0)
@@ -375,13 +360,9 @@
     def from_z(i):
         return lax.rem(z + NZ - far_first(i), NZ)
 
-    def agy_copy(i, n):
+    def agy_copy(i, dy):
         part = piece(from_z(i), y)
-        return copy(part, part, agy_s.at[i, n], agy_r.at[i, n], dev(dy=(near, back)[n]))
-
-    def agf_copy(i):
-        part = piece(from_z(i), lax.rem(y + back, NY))
-        return copy(part, part, agf_s.at[i], agf_r.at[i], dev(dy=near))
+        return copy(part, part, agy_s.at[i, dy - 1], agy_r.at[i, dy - 1], dev(dy=dy))
 
     def agc_copy(i):
         zz = from_z(i)
@@ -392,7 +373,8 @@
         agz_copy(i).start()
         return carry
 
-    lax.fori_loop(0, NZ - 1, gather_z, 0)
+    gather_z(0, 0)
+    lax.fori_loop(0, NZ - 2, lambda n, carry: gather_z(NZ - 2 - n, carry), 0)
 
     def gather(n, carry):
         @pl.when(n < NZ)
@@ -403,35 +385,27 @@
             def _():
                 agz_copy(i).wait_recv()
 
-            agy_copy(i, 0).start()
-            agy_copy(i, 1).start()
-
-        @pl.when((n >= G_LAG) & (n < NZ + G_LAG))
+            for dy in (2, 1, 3):
+                agy_copy(i, dy).start()
+
+        @pl.when(n >= G_LAG)
         def _():
             i = NZ - 1 - (n - G_LAG)
-            agy_copy(i, 0).wait_recv()
-            agf_copy(i).start()
-
-        @pl.when(n >= 2 * G_LAG)
-        def _():
-            i = NZ - 1 - (n - 2 * G_LAG)
-            agy_copy(i, 1).wait_recv()
-            agf_copy(i).wait_recv()
+            for dy in (1, 3, 2):
+                agy_copy(i, dy).wait_recv()
             agc_copy(i).start()
 
         return carry
 
-    lax.fori_loop(0, NZ + 2 * G_LAG, gather, 0)
+    lax.fori_loop(0, NZ + G_LAG, gather, 0)
 
     def finish(i, carry):
         agc_copy(i).wait_recv()
         agc_copy(i).wait_send()
         core_copy(i).wait_send()
-        relay_copy(i).wait_send()
-        agf_copy(i).wait_send()
-        for n in range(2):
-            y_copy(i, n).wait_send()
-            agy_copy(i, n).wait_send()
+        for dy in (1, 2, 3):
+            y_copy(i, dy).wait_send()
+            agy_copy(i, dy).wait_send()
 
         @pl.when(i < NZ - 1)
         def _():
@@ -462,16 +436,19 @@
             vm((T, NY * NZ, NZ, LANES), f32), vm((T, 2, NZ, LANES), f32),
             vm((T, CHUNKS, LANES), f32), vm((T, NX, CHUNKS, LANES), f32),
             vm((2 * GROUP, R), jnp.bfloat16), vm((NZ, 2, GROUP, D), f32), vm((NZ, GROUP, D), f32),
-            vm((NZ, SHARD, D), f32), vm((NZ, 2, SHARD, D), f32), vm((NZ, SHARD, D), f32), vm((NZ - 1, SHARD, D), f32),
+            vm((NZ, NY - 1, SHARD, D), f32), vm((NZ, SHARD, D), f32), vm((NZ - 1, SHARD, D), f32),
             dma((T,)), dma((T,)), dma((T, NY * NZ)), dma((T, NY * NZ)), dma((T,)), dma((T,)),
             dma((T, NX - 1)), dma((T, NX - 1)),
-            dma((NZ,)), dma((NZ,)), dma((NZ,)), dma((NZ,)), dma((NZ, 2)), dma((NZ, 2)), dma((NZ,)), dma((NZ,)),
-            dma((NZ,)), dma((NZ,)), dma((NZ, 2)), dma((NZ, 2)), dma((NZ,)), dma((NZ,)), dma((NZ,)), dma((NZ,)),
+            dma((NZ,)), dma((NZ,)), dma((NZ, NY - 1)), dma((NZ, NY - 1)), dma((NZ,)), dma((NZ,)),
+            dma((NZ,)), dma((NZ,)), dma((NZ, NY - 1)), dma((NZ, NY - 1)), dma((NZ,)), dma((NZ,)),
         ],
         compiler_params=pltpu.CompilerParams(
             collective_id=0, has_side_effects=True, vmem_limit_bytes=48 << 20
         ),
-    )(patients, centroids)
+    )(
+        pltpu.with_memory_space_constraint(patients, pltpu.HBM),
+        pltpu.with_memory_space_constraint(centroids, pltpu.HBM),
+    )
     return new, log.reshape(R)
 
 

time: 114 us -> 107 us (0.939)
  Pallas kernels: 109 us -> 104 us
  local copies, waits for them, and re-layouts: 4.36 us -> 1.92 us
    pallas_call x1, Pallas kernels: 109 us -> 104 us  [local(): pl.pallas_call(functools.partial(kernel, ratio), out_shape=(jax.ShapeDtyp...]
    unnamed x6 -> x2, local copies, waits for them, and re-layouts: 4.36 us -> 1.92 us
where the time goes in v3:
time: 107 us
  Pallas kernels  104 us (97%)
  local copies, waits for them, and re-layouts  1.92 us (2%)
    pallas_call x1, Pallas kernels, local(): pl.pallas_call(functools.partial(kernel, ratio), out_shape=(jax.ShapeDtyp...  104 us

profile of v3, /device:TPU:1, one launch (start us, length us, event | category | flops | bytes accessed | tf_op | source)
XLA Modules:
  0.0 106.8 jit_solution(17455495732264396774)
XLA Ops:
  0.6 104.2 %shard_map.41 = (f32[2048,256]{1,0:T(8,128)S(1)}, f32[16,128]{1,0:T(8,128)S(1)}) custom-call(bf16[2048,256]{1,0:T(8,128)(2,1)} %p_hbm.1, bf16[2048,256]{1,0:T(8,128)(2,1)} %c_hbm.1), custom_call_target="tpu_custom_call" | custom-call | tf_op jit(solution)/shard_map/pallas_call | solution.py:426
  104.9 1.3 %copy.6 = f32[2048,256]{1,0:T(8,128)} copy(f32[2048,256]{1,0:T(8,128)S(1)} %get-tuple-element.8) | data formatting | bytes 4194304
  106.2 0.6 copy.7

commit v4 on v3

--- a/solution.py
+++ b/solution.py
@@ -25,6 +25,9 @@
 Y_LAG = 7
 G_LAG = 4
 NT = (((1,), (1,)), ((), ()))
+
+
+PEERS = [(dy, dz) for dz in (4, 3, 5, 2, 6, 1, 7, 0) for dy in (2, 1, 3, 0)][:-1]
 
 
 def far_first(i):
@@ -65,18 +68,8 @@
 
     barrier = pltpu.get_barrier_semaphore()
 
-    def greet(i, carry):
-        dz = far_first(i)
-        for dy in (2, 1, 3):
-            pl.semaphore_signal(barrier, inc=1, device_id=dev(dy=dy, dz=dz), device_id_type=MESH)
-
-        @pl.when(i < NZ - 1)
-        def _():
-            pl.semaphore_signal(barrier, inc=1, device_id=dev(dz=dz), device_id_type=MESH)
-
-        return carry
-
-    lax.fori_loop(0, NZ, greet, 0)
+    for dy, dz in PEERS:
+        pl.semaphore_signal(barrier, inc=1, device_id=dev(dy=dy, dz=dz), device_id_type=MESH)
     for dx in (2, 1, 3):
         pl.semaphore_signal(barrier, inc=1, device_id=dev(dx=dx), device_id_type=MESH)
     pl.semaphore_signal(barrier, inc=1, device_id=dev(flip=True), device_id_type=MESH)
@@ -143,7 +136,7 @@
     to_dense(peak8, rowpart.at[0])
     pl.semaphore_wait(barrier, NY * NZ - 1 + NX - 1 + 1)
 
-    def x_exchange(t):
+    def x_exchange(t, meanwhile=lambda: None):
         xbuf[t, x] = rowpart[t]
 
         def one(dx):
@@ -151,10 +144,11 @@
 
         for dx in (2, 1, 3):
             one(dx).start()
+        meanwhile()
+        for dx in (1, 3, 2):
+            one(dx).wait_send()
         for dx in (1, 3, 2):
             one(dx).wait_recv()
-        for dx in (1, 3, 2):
-            one(dx).wait_send()
 
     x_exchange(0)
     peak = jnp.maximum(jnp.maximum(xbuf[0, 0], xbuf[0, 1]), jnp.maximum(xbuf[0, 2], xbuf[0, 3]))
@@ -198,35 +192,24 @@
     def post_copy(t):
         return copy(total.at[t, core], total.at[t, core], post_s.at[t], post_r.at[t], dev(flip=True))
 
-    def col_copy(t, i, dy):
-        k = i * NY + dy
-        return copy(own.at[t], colbuf.at[t, k], col_s.at[t, k], col_r.at[t, k], dev(dy=dy, dz=far_first(i)))
-
-    def each_peer(act):
-        def body(i, carry):
-            for dy in (2, 1, 3):
-                act(i, dy)
-
-            @pl.when(i < NZ - 1)
-            def _():
-                act(i, 0)
-
-            return carry
-
-        lax.fori_loop(0, NZ, body, 0)
+    def col_all(t):
+        return copy(colbuf.at[t], colbuf.at[t], col_s.at[t], col_r.at[t], dev(dz=1))
 
     def col_send(t):
         pre_copy(t).wait_recv()
         own[t] = dense[t, core] + pre[t]
-        each_peer(lambda i, dy: col_copy(t, i, dy).start())
+        for k, (dy, dz) in enumerate(PEERS):
+            copy(own.at[t], colbuf.at[t, k], col_s.at[t], col_r.at[t], dev(dy=dy, dz=dz)).start()
 
     def col_finish(t):
-        each_peer(lambda i, dy: col_copy(t, i, dy).wait_recv())
-        terms = [colbuf[t, k] for k in range(NY * NZ) if k != NY * (NZ - 1)] + [own[t]]
+        col_all(t).wait_recv()
+        terms = [colbuf[t, k] for k in range(len(PEERS))] + [own[t]]
         while len(terms) > 1:
             terms = [a + b for a, b in zip(terms[::2], terms[1::2])]
         total[t, core] = terms[0]
-        each_peer(lambda i, dy: col_copy(t, i, dy).wait_send())
+
+    def col_drain(t):
+        col_all(t).wait_send()
         pre_copy(t).wait_send()
 
     def scale_half(t, h):
@@ -252,11 +235,15 @@
         for g in range(CHUNKS):
             rowpart[t + 1, g : g + 1, :] = jnp.sum(mass[g], axis=0, keepdims=True)
         rowpart[t + 1] = rowpart[t + 1] * factor[...]
-        x_exchange(t + 1)
+
+        def drain():
+            col_drain(t)
+            post_copy(t).wait_send()
+
+        x_exchange(t + 1, drain)
         row_mass = (xbuf[t + 1, 0] + xbuf[t + 1, 1]) + (xbuf[t + 1, 2] + xbuf[t + 1, 3])
         log_ref[...] = -jnp.log(row_mass)
         to_lanes(factor[...] / row_mass, row_b)
-        post_copy(t).wait_send()
         return carry
 
     lax.fori_loop(0, ITERS, one_round, 0)
@@ -329,13 +316,14 @@
     lane_sums(other, ITERS)
     pre_copy(ITERS).start()
     lane_sums(core, ITERS)
+    z_step(NZ + 2 - Y_LAG)
     col_send(ITERS)
 
     def scatter(i, carry):
         z_step(i)
         return carry
 
-    lax.fori_loop(NZ + 2 - Y_LAG, NZ, scatter, 0)
+    lax.fori_loop(NZ + 3 - Y_LAG, NZ, scatter, 0)
 
     col_finish(ITERS)
     weight = jnp.maximum(total[ITERS, core, pl.ds(z, 1), :], 1.0)
@@ -367,7 +355,7 @@
     def agc_copy(i):
         zz = from_z(i)
         part = new_ref.at[pl.ds(pl.multiple_of(core * HALF + zz * GROUP, GROUP), GROUP)]
-        return copy(part, part, agc_s.at[i], agc_r.at[i], dev(flip=True))
+        return copy(part, part, agc_s.at[0], agc_r.at[0], dev(flip=True))
 
     def gather_z(i, carry):
         agz_copy(i).start()
@@ -376,15 +364,23 @@
     gather_z(0, 0)
     lax.fori_loop(0, NZ - 2, lambda n, carry: gather_z(NZ - 2 - n, carry), 0)
 
+    def drain_scatter(i, carry):
+        core_copy(i).wait_send()
+        for dy in (1, 2, 3):
+            y_copy(i, dy).wait_send()
+
+        @pl.when(i < NZ - 1)
+        def _():
+            z_copy(i).wait_send()
+
+        return carry
+
     def gather(n, carry):
         @pl.when(n < NZ)
         def _():
             i = NZ - 1 - n
 
-            @pl.when(n > 0)
-            def _():
-                agz_copy(i).wait_recv()
-
+            agz_copy(i).wait_recv()
             for dy in (2, 1, 3):
                 agy_copy(i, dy).start()
 
@@ -397,24 +393,27 @@
 
         return carry
 
-    lax.fori_loop(0, NZ + G_LAG, gather, 0)
-
-    def finish(i, carry):
-        agc_copy(i).wait_recv()
-        agc_copy(i).wait_send()
-        core_copy(i).wait_send()
+    for dy in (2, 1, 3):
+        agy_copy(NZ - 1, dy).start()
+    col_drain(ITERS)
+    lax.fori_loop(0, NZ, drain_scatter, 0)
+    lax.fori_loop(1, NZ + G_LAG, gather, 0)
+
+    def drain_gather(i, carry):
         for dy in (1, 2, 3):
-            y_copy(i, dy).wait_send()
             agy_copy(i, dy).wait_send()
 
         @pl.when(i < NZ - 1)
         def _():
-            z_copy(i).wait_send()
             agz_copy(i).wait_send()
 
         return carry
 
-    lax.fori_loop(0, NZ, finish, 0)
+    lax.fori_loop(0, NZ, drain_gather, 0)
+    half = new_ref.at[pl.ds(pl.multiple_of(core * HALF, HALF), HALF)]
+    whole = copy(half, half, agc_s.at[0], agc_r.at[0], dev(flip=True))
+    whole.wait_send()
+    whole.wait_recv()
 
 
 def local(patients, centroids):
@@ -433,14 +432,14 @@
             vm((K, R), f32), vm((K, LANES), f32), vm((8, R), f32), vm((K, LANES), f32), vm((K, LANES), f32),
             vm((8, R), f32), vm((CHUNKS, LANES), f32),
             vm((T, 2, NZ, LANES), f32), vm((T, NZ, LANES), f32), vm((T, NZ, LANES), f32),
-            vm((T, NY * NZ, NZ, LANES), f32), vm((T, 2, NZ, LANES), f32),
+            vm((T, NY * NZ - 1, NZ, LANES), f32), vm((T, 2, NZ, LANES), f32),
             vm((T, CHUNKS, LANES), f32), vm((T, NX, CHUNKS, LANES), f32),
             vm((2 * GROUP, R), jnp.bfloat16), vm((NZ, 2, GROUP, D), f32), vm((NZ, GROUP, D), f32),
             vm((NZ, NY - 1, SHARD, D), f32), vm((NZ, SHARD, D), f32), vm((NZ - 1, SHARD, D), f32),
-            dma((T,)), dma((T,)), dma((T, NY * NZ)), dma((T, NY * NZ)), dma((T,)), dma((T,)),
+            dma((T,)), dma((T,)), dma((T,)), dma((T,)), dma((T,)), dma((T,)),
             dma((T, NX - 1)), dma((T, NX - 1)),
             dma((NZ,)), dma((NZ,)), dma((NZ, NY - 1)), dma((NZ, NY - 1)), dma((NZ,)), dma((NZ,)),
-            dma((NZ,)), dma((NZ,)), dma((NZ, NY - 1)), dma((NZ, NY - 1)), dma((NZ,)), dma((NZ,)),
+            dma((NZ,)), dma((NZ,)), dma((NZ, NY - 1)), dma((NZ, NY - 1)), dma((1,)), dma((1,)),
         ],
         compiler_params=pltpu.CompilerParams(
             collective_id=0, has_side_effects=True, vmem_limit_bytes=48 << 20

time: 107 us -> 103 us (0.963)
  Pallas kernels: 104 us -> 101 us
    pallas_call x1, Pallas kernels: 104 us -> 101 us  [local(): pl.pallas_call(functools.partial(kernel, ratio), out_shape=(jax.ShapeDtyp...]
where the time goes in v4:
time: 103 us
  Pallas kernels  101 us (98%)
  local copies, waits for them, and re-layouts  1.92 us (2%)
    pallas_call x1, Pallas kernels, local(): pl.pallas_call(functools.partial(kernel, ratio), out_shape=(jax.ShapeDtyp...  101 us

profile of v4, /device:TPU:1, one launch (start us, length us, event | category | flops | bytes accessed | tf_op | source)
XLA Modules:
  0.0 103.3 jit_solution(1900130507575997209)
XLA Ops:
  0.6 100.7 %shard_map.41 = (f32[2048,256]{1,0:T(8,128)S(1)}, f32[16,128]{1,0:T(8,128)S(1)}) custom-call(bf16[2048,256]{1,0:T(8,128)(2,1)} %p_hbm.1, bf16[2048,256]{1,0:T(8,128)(2,1)} %c_hbm.1), custom_call_target="tpu_custom_call" | custom-call | tf_op jit(solution)/shard_map/pallas_call | solution.py:425
  101.3 1.3 %copy.6 = f32[2048,256]{1,0:T(8,128)} copy(f32[2048,256]{1,0:T(8,128)S(1)} %get-tuple-element.8) | data formatting | bytes 4194304
  102.7 0.6 copy.7

commit v5 on v4

--- a/solution.py
+++ b/solution.py
@@ -23,7 +23,7 @@
 CHUNKS = R // LANES
 MESH = pl.DeviceIdType.MESH
 Y_LAG = 7
-G_LAG = 4
+G_LAG = 5
 NT = (((1,), (1,)), ((), ()))
 
 
@@ -155,15 +155,10 @@
     factor[...] = jnp.exp2(rowpart[0] - peak)
     to_lanes(factor[...], row_b)
 
-    ones = jnp.ones((8, LANES), jnp.float32)
-
     def lane_sums(h, t):
         for g in range(NZ):
             at = pl.ds(pl.multiple_of(h * HALF + g * LANES, LANES), LANES)
-            s = lax.dot_general(
-                ones, acc[at, :], NT, preferred_element_type=jnp.float32, precision=lax.Precision.HIGHEST
-            )
-            dense[t, h, g : g + 1, :] = s[0:1, :]
+            dense[t, h, g : g + 1, :] = jnp.sum(acc[at, :].T, axis=0, keepdims=True)
 
     def col_pass(h):
         r = [row_b[:, k * LANES : (k + 1) * LANES] for k in range(CHUNKS)]
@@ -291,7 +286,7 @@
                     acc[at, :] = terms[0]
                     return carry
 
-                lax.fori_loop(0, GROUP // 16, body, 0, unroll=2)
+                lax.fori_loop(0, GROUP // 16, body, 0, unroll=4)
             both = jnp.dot(low[...], p_ref[...], preferred_element_type=jnp.float32)
             numer[i, 0] = both[:GROUP]
             numer[i, 1] = both[GROUP:]

time: 103 us -> 100 us (0.971)
  Pallas kernels: 101 us -> 97.7 us
    pallas_call x1, Pallas kernels: 101 us -> 97.7 us  [local(): pl.pallas_call(functools.partial(kernel, ratio), out_shape=(jax.ShapeDtyp...]
where the time goes in v5:
time: 100 us
  Pallas kernels  97.7 us (98%)
  local copies, waits for them, and re-layouts  1.92 us (2%)
    pallas_call x1, Pallas kernels, local(): pl.pallas_call(functools.partial(kernel, ratio), out_shape=(jax.ShapeDtyp...  97.7 us

profile of v5, /device:TPU:1, one launch (start us, length us, event | category | flops | bytes accessed | tf_op | source)
XLA Modules:
  0.0 100.3 jit_solution(1749877797290689397)
XLA Ops:
  0.6 97.7 %shard_map.41 = (f32[2048,256]{1,0:T(8,128)S(1)}, f32[16,128]{1,0:T(8,128)S(1)}) custom-call(bf16[2048,256]{1,0:T(8,128)(2,1)} %p_hbm.1, bf16[2048,256]{1,0:T(8,128)(2,1)} %c_hbm.1), custom_call_target="tpu_custom_call" | custom-call | tf_op jit(solution)/shard_map/pallas_call | solution.py:420
  98.3 1.3 %copy.6 = f32[2048,256]{1,0:T(8,128)} copy(f32[2048,256]{1,0:T(8,128)S(1)} %get-tuple-element.8) | data formatting | bytes 4194304
  99.7 0.6 copy.7

commit v6 on v5

--- a/solution.py
+++ b/solution.py
@@ -39,8 +39,8 @@
     ratio, p_hbm, c_hbm, new_ref, log_ref, p_ref, c_ref, t_even, t_odd, in_s,
     expo, col_b, row_b, acc, norm_b, peak8, factor,
     dense, pre, own, colbuf, total, rowpart, xbuf,
-    low, numer, corebuf, ybuf, zsrc, zbuf,
-    pre_s, pre_r, col_s, col_r, post_s, post_r, x_s, x_r,
+    low, numer, corebuf, ybuf, zsrc, zbuf, w_rows, w_buf,
+    pre_s, pre_r, col_s, col_r, w_s, w_r, post_s, post_r, x_s, x_r,
     core_s, core_r, y_s, y_r, z_s, z_r, agz_s, agz_r, agy_s, agy_r, agc_s, agc_r,
 ):
     x = lax.axis_index("cents")
@@ -311,17 +311,27 @@
     lane_sums(other, ITERS)
     pre_copy(ITERS).start()
     lane_sums(core, ITERS)
-    z_step(NZ + 2 - Y_LAG)
-    col_send(ITERS)
+    for i in range(NZ + 2 - Y_LAG, NZ + 4 - Y_LAG):
+        z_step(i)
+    pre_copy(ITERS).wait_recv()
+    weights = dense[ITERS, core] + pre[ITERS]
+    for g in range(NZ):
+        w_rows[g] = weights[g : g + 1, :]
+    for k, (dy, dz) in enumerate(PEERS):
+        copy(w_rows.at[lax.rem(z + dz, NZ)], w_buf.at[k], w_s, w_r, dev(dy=dy, dz=dz)).start()
+    w_all = copy(w_buf, w_buf, w_s, w_r, dev(dz=1))
 
     def scatter(i, carry):
         z_step(i)
         return carry
 
-    lax.fori_loop(NZ + 3 - Y_LAG, NZ, scatter, 0)
-
-    col_finish(ITERS)
-    weight = jnp.maximum(total[ITERS, core, pl.ds(z, 1), :], 1.0)
+    lax.fori_loop(NZ + 4 - Y_LAG, NZ, scatter, 0)
+
+    w_all.wait_recv()
+    weight = w_rows[z]
+    for k in range(len(PEERS)):
+        weight = weight + w_buf[k]
+    weight = jnp.maximum(weight, 1.0)
     norm_b[0:LANES, :] = jnp.broadcast_to(weight, (LANES, LANES)).T
 
     for i in range(NZ - 1):
@@ -390,7 +400,8 @@
 
     for dy in (2, 1, 3):
         agy_copy(NZ - 1, dy).start()
-    col_drain(ITERS)
+    w_all.wait_send()
+    pre_copy(ITERS).wait_send()
     lax.fori_loop(0, NZ, drain_scatter, 0)
     lax.fori_loop(1, NZ + G_LAG, gather, 0)
 
@@ -431,7 +442,8 @@
             vm((T, CHUNKS, LANES), f32), vm((T, NX, CHUNKS, LANES), f32),
             vm((2 * GROUP, R), jnp.bfloat16), vm((NZ, 2, GROUP, D), f32), vm((NZ, GROUP, D), f32),
             vm((NZ, NY - 1, SHARD, D), f32), vm((NZ, SHARD, D), f32), vm((NZ - 1, SHARD, D), f32),
-            dma((T,)), dma((T,)), dma((T,)), dma((T,)), dma((T,)), dma((T,)),
+            vm((NZ, 1, LANES), f32), vm((NY * NZ - 1, 1, LANES), f32),
+            dma((T,)), dma((T,)), dma((T,)), dma((T,)), dma, dma, dma((T,)), dma((T,)),
             dma((T, NX - 1)), dma((T, NX - 1)),
             dma((NZ,)), dma((NZ,)), dma((NZ, NY - 1)), dma((NZ, NY - 1)), dma((NZ,)), dma((NZ,)),
             dma((NZ,)), dma((NZ,)), dma((NZ, NY - 1)), dma((NZ, NY - 1)), dma((1,)), dma((1,)),

time: 100 us -> 98.5 us (0.985)
  Pallas kernels: 97.7 us -> 95.8 us
    pallas_call x1, Pallas kernels: 97.7 us -> 95.8 us  [local(): pl.pallas_call(functools.partial(kernel, ratio), out_shape=(jax.ShapeDtyp...]
where the time goes in v6:
time: 98.5 us; the launch traced here: 98.4 us
  Pallas kernels  95.8 us (97%)
  local copies, waits for them, and re-layouts  1.92 us (2%)
    pallas_call x1, Pallas kernels, local(): pl.pallas_call(functools.partial(kernel, ratio), out_shape=(jax.ShapeDtyp...  95.8 us

profile of v6, /device:TPU:1, one launch (start us, length us, event | category | flops | bytes accessed | tf_op | source)
XLA Modules:
  0.0 98.4 jit_solution(5193166772840261572)
XLA Ops:
  0.6 95.8 %shard_map.41 = (f32[2048,256]{1,0:T(8,128)S(1)}, f32[16,128]{1,0:T(8,128)S(1)}) custom-call(bf16[2048,256]{1,0:T(8,128)(2,1)} %p_hbm.1, bf16[2048,256]{1,0:T(8,128)(2,1)} %c_hbm.1), custom_call_target="tpu_custom_call" | custom-call | tf_op jit(solution)/shard_map/pallas_call | solution.py:431
  96.5 1.3 %copy.6 = f32[2048,256]{1,0:T(8,128)} copy(f32[2048,256]{1,0:T(8,128)S(1)} %get-tuple-element.8) | data formatting | bytes 4194304
  97.8 0.6 copy.7

commit v7 on v6

--- a/solution.py
+++ b/solution.py
@@ -237,11 +237,12 @@
 
         x_exchange(t + 1, drain)
         row_mass = (xbuf[t + 1, 0] + xbuf[t + 1, 1]) + (xbuf[t + 1, 2] + xbuf[t + 1, 3])
-        log_ref[...] = -jnp.log(row_mass)
+        log_ref[...] = row_mass
         to_lanes(factor[...] / row_mass, row_b)
         return carry
 
     lax.fori_loop(0, ITERS, one_round, 0)
+    log_ref[...] = -jnp.log(log_ref[...])
 
     def core_copy(i):
         return copy(numer.at[i, 1], corebuf.at[i], core_s.at[i], core_r.at[i], dev(flip=True))

time: 98.5 us -> 98.5 us (level)
  no operation moved by 1% of the time
where the time goes in v7:
time: 98.5 us; the launch traced here: 98.4 us
  Pallas kernels  95.8 us (97%)
  local copies, waits for them, and re-layouts  1.92 us (2%)
    pallas_call x1, Pallas kernels, local(): pl.pallas_call(functools.partial(kernel, ratio), out_shape=(jax.ShapeDtyp...  95.8 us

profile of v7, /device:TPU:1, one launch (start us, length us, event | category | flops | bytes accessed | tf_op | source)
XLA Modules:
  0.0 98.4 jit_solution(334655082885835017)
XLA Ops:
  0.6 95.8 %shard_map.41 = (f32[2048,256]{1,0:T(8,128)S(1)}, f32[16,128]{1,0:T(8,128)S(1)}) custom-call(bf16[2048,256]{1,0:T(8,128)(2,1)} %p_hbm.1, bf16[2048,256]{1,0:T(8,128)(2,1)} %c_hbm.1), custom_call_target="tpu_custom_call" | custom-call | tf_op jit(solution)/shard_map/pallas_call | solution.py:432
  96.4 1.3 %copy.6 = f32[2048,256]{1,0:T(8,128)} copy(f32[2048,256]{1,0:T(8,128)S(1)} %get-tuple-element.8) | data formatting | bytes 4194304
  97.8 0.6 copy.7
